TPU v7x, 32 devices: a whole 2x2x4 slice. The times are simulated.
32 devices in a mesh: dp: 4 (over y, x), row: 4 (over z), col: 2 (over core).
Axes of the slice: x: 2, y: 2, z: 4, core: 2. Of those that a mesh axis runs over, the one named last changes fastest.
Arguments:
- x_in: bfloat16 [1024, 1536], P(('dp', 'col'), 'row'), may hold values from -6 to 6
- lengths: int32 [4, 8], replicated, may hold values from 1 to 128, 256 in all within a row
- seq_order: int32 [32], replicated, may hold values from 0 to 31, each once
- norm1_gain: float32 [1536], P('row'), may hold values from 0.5 to 1.5
- w_in_x: bfloat16 [1536, 3072], P('row', 'col'), may hold values from -0.15625 to 0.15625
- w_in_z: bfloat16 [1536, 3072], P('row', 'col'), may hold values from -0.15625 to 0.15625
- conv_w: float32 [3072, 4], P(('col', 'row')), may hold values from -0.5 to 0.5
- conv_b: float32 [3072], P(('col', 'row')), may hold values from -0.5 to 0.5
- w_xp: bfloat16 [3072, 128], P(('col', 'row')), may hold values from -0.109375 to 0.109375
- w_dt: bfloat16 [96, 3072], P(None, ('col', 'row')), may hold values from -0.625 to 0.625
- dt_bias: float32 [3072], P(('col', 'row')), may hold values from -6.9 to -2.3
- a_log: float32 [3072, 16], P(('col', 'row')), may hold values from 0 to 2.77
- skip_weight: float32 [3072], P(('col', 'row')), may hold values from 0.5 to 1.5
- w_out: bfloat16 [3072, 1536], P('col', 'row'), may hold values from -0.109375 to 0.109375
- norm2_gain: float32 [1536], P('row'), may hold values from 0.5 to 1.5
- w_gate: bfloat16 [1536, 4096], P('row', 'col'), may hold values from -0.15625 to 0.15625
- w_up: bfloat16 [1536, 4096], P('row', 'col'), may hold values from -0.15625 to 0.15625
- w_down: bfloat16 [4096, 1536], P('col', 'row'), may hold values from -0.09375 to 0.09375
- cotangent: bfloat16 [1024, 1536], P(('dp', 'col'), 'row'), may hold values from -6 to 6
Outputs:
- y_out: bfloat16 [1024, 1536], P(('dp', 'col'), 'row')
- dx_out: bfloat16 [1024, 1536], P(('dp', 'col'), 'row')
- grad_norm1_gain: float32 [1536], P('row')
- grad_w_in_x: float32 [1536, 3072], P('row', 'col')
- grad_w_in_z: float32 [1536, 3072], P('row', 'col')
- grad_conv_w: float32 [3072, 4], P(('col', 'row'))
- grad_conv_b: float32 [3072], P(('col', 'row'))
- grad_w_xp: float32 [3072, 128], P(('col', 'row'))
- grad_w_dt: float32 [96, 3072], P(None, ('col', 'row'))
- grad_dt_bias: float32 [3072], P(('col', 'row'))
- grad_a_log: float32 [3072, 16], P(('col', 'row'))
- grad_skip_weight: float32 [3072], P(('col', 'row'))
- grad_w_out: float32 [3072, 1536], P('col', 'row')
- grad_norm2_gain: float32 [1536], P('row')
- grad_w_gate: float32 [1536, 4096], P('row', 'col')
- grad_w_up: float32 [1536, 4096], P('row', 'col')
- grad_w_down: float32 [4096, 1536], P('col', 'row')
Inputs may be any that keep to these rules, and one draw needn't show every extreme that they name: Each row of lengths holds the lengths of one group's 8 sequences and sums to 256. `seq_order`: A permutation of the 32 sequence numbers.
All inputs are finite; a program needn't handle non-finite values.
Results may differ from a plain program's by a relative error of at most 0.015.
Values may be sent and summed in bfloat16 or wider, within the bound.
A program may use at most 192 MiB of HBM per device.

v0:
```python
import functools

import jax
import jax.numpy as jnp
from jax import lax
from jax.experimental import pallas as pl
from jax.experimental.pallas import tpu as pltpu
from jax.sharding import PartitionSpec as P

epsilon = 1e-05


def layout(lengths, seq_order, group_rows):
    flat_lengths = lengths.reshape(-1)
    total_seqs = flat_lengths.shape[0]
    slot_length = jnp.take(flat_lengths, seq_order)
    input_start = jnp.cumsum(slot_length) - slot_length
    slot_of = (
        jnp.zeros((total_seqs,), jnp.int32)
        .at[seq_order]
        .set(jnp.arange(total_seqs, dtype=jnp.int32))
    )
    seq_input = jnp.take(input_start, slot_of).reshape(lengths.shape)
    group_start = jnp.cumsum(lengths, axis=1) - lengths
    places = jnp.arange(group_rows, dtype=jnp.int32)
    member = (
        jnp.sum((places[None, :, None] >= group_start[:, None, :]).astype(jnp.int32), axis=2) - 1
    )
    begin_at = jnp.take_along_axis(group_start, member, axis=1)
    within = places[None, :] - begin_at
    source = jnp.take_along_axis(seq_input, member, axis=1) + within
    return (source, within)


def silu_slope(values):
    sigmoid_v = jax.nn.sigmoid(values)
    return sigmoid_v * (1.0 + values * (1.0 - sigmoid_v))


def contract(left, right, left_dim, right_dim):
    return lax.dot_general(
        left, right, (((left_dim,), (right_dim,)), ((), ())), preferred_element_type=jnp.float32
    )


def convolve(inner_x, kernel, kernel_bias, places):
    tap_count = kernel.shape[1]
    conv_sum = kernel_bias[:, None] + inner_x * kernel[:, tap_count - 1][:, None]
    for shift_by in range(1, tap_count):
        shifted = jnp.pad(inner_x, ((0, 0), (shift_by, 0)))[:, :-shift_by]
        conv_sum = (
            conv_sum
            + shifted
            * (places >= shift_by).astype(jnp.float32)[None, :]
            * kernel[:, tap_count - 1 - shift_by][:, None]
        )
    return jax.nn.silu(conv_sum)


MESH = pl.DeviceIdType.MESH
f32 = jnp.float32
bf16 = jnp.bfloat16


def remote(src, dst, send, recv, where):
    return pltpu.make_async_remote_copy(
        src_ref=src, dst_ref=dst, send_sem=send, recv_sem=recv, device_id=where, device_id_type=MESH
    )


def away(axis, offset):
    return {axis: lax.rem(lax.axis_index(axis) + offset, lax.axis_size(axis))}


def greet(*axes):
    barrier = pltpu.get_barrier_semaphore()
    total = 0
    for axis in axes:
        for offset in range(1, lax.axis_size(axis)):
            pl.semaphore_signal(barrier, inc=1, device_id=away(axis, offset), device_id_type=MESH)
            total += 1
    return lambda: pl.semaphore_wait(barrier, total)


class Late:
    def __init__(self, names, sources, targets, sems):
        self.targets = dict(zip(names, targets))
        self.waiting = {}
        for i, (name, source, target) in enumerate(zip(names, sources, targets)):
            self.waiting[name] = pltpu.make_async_copy(source, target, sems.at[i])
            self.waiting[name].start()

    def __call__(self, name):
        if name in self.waiting:
            self.waiting.pop(name).wait()
        return self.targets[name]


class Leave:
    def __init__(self, names, sources, targets, sems):
        self.copies = {
            name: pltpu.make_async_copy(source, target, sems.at[i])
            for i, (name, source, target) in enumerate(zip(names, sources, targets))
        }

    def __call__(self, *names):
        for name in names:
            self.copies[name].start()

    def finish(self):
        for copy in self.copies.values():
            copy.wait()


def matmul(left, right):
    return jnp.dot(left, right, preferred_element_type=f32)


def silu(values):
    return values * jax.nn.sigmoid(values)


def rows_form(values):
    ones = jnp.ones((8, values.shape[1]), f32)
    return lax.dot_general(
        ones,
        values,
        (((1,), (1,)), ((), ())),
        precision=lax.Precision.HIGHEST,
        preferred_element_type=f32,
    )


def column_form(row_values):
    return jnp.transpose(row_values)[:, 0:1]


class Line:
    def __init__(self, axis, send, recv):
        self.axis, self.send, self.recv = axis, send, recv
        self.size = lax.axis_size(axis)
        self.me = lax.axis_index(axis)

    def right(self, src, dst, d):
        return remote(
            src, dst, self.send.at[0, d], self.recv.at[0, d], {self.axis: jnp.minimum(self.me + 1, self.size - 1)}
        )

    def left(self, src, dst, d):
        return remote(
            src, dst, self.send.at[1, d], self.recv.at[1, d], {self.axis: jnp.maximum(self.me - 1, 0)}
        )


def line_gather(axis, slot_of, send, recv):
    line = Line(axis, send, recv)
    size, me = line.size, line.me
    last = size - 1

    def go_right(s):
        slot = jnp.maximum(me - s, 0)
        return (me - s >= 0) & (me < last), line.right(slot_of(slot), slot_of(slot), slot)

    def go_left(s):
        slot = jnp.minimum(me + s, last)
        return (me + s <= last) & (me > 0), line.left(slot_of(slot), slot_of(slot), slot)

    for s in range(last):
        for valid, copy in (go_right(s), go_left(s)):
            pl.when(valid)(copy.start)
        yield
        slot = jnp.maximum(me - 1 - s, 0)
        pl.when(me - 1 - s >= 0)(line.right(slot_of(slot), slot_of(slot), slot).wait_recv)
        slot = jnp.minimum(me + 1 + s, last)
        pl.when(me + 1 + s <= last)(line.left(slot_of(slot), slot_of(slot), slot).wait_recv)
    yield
    for s in range(last):
        for valid, copy in (go_right(s), go_left(s)):
            pl.when(valid)(copy.wait_send)


def line_scatter(axis, block_of, out, held, from_left, from_right, send, recv, slots=False):
    line = Line(axis, send, recv)
    size, me = line.size, line.me
    last = size - 1

    def right_at(t):
        d = jnp.clip(last - t + me, 0, last)
        return (t >= me) & (me < last), d, line.right(held.at[d], from_left.at[d], d)

    def left_at(t):
        d = jnp.clip(t - (last - me), 0, last)
        return (t >= last - me) & (me > 0), d, line.left(held.at[d], from_right.at[d], d)

    def made(d, slot):
        return block_of(d, slot) if slots else block_of(d)

    def pass_on(valid, first, d, copy, arrived, slot):
        @pl.when(valid)
        def _():
            part = made(d, slot)

            @pl.when(jnp.logical_not(first))
            def _():
                copy.wait_recv()
                held[d] = (part + arrived[d].astype(f32)).astype(held.dtype)

            @pl.when(first)
            def _():
                held[d] = part.astype(held.dtype)

            copy.start()

    for t in range(last):
        valid, d, copy = right_at(t)
        pass_on(valid, me == 0, d, copy, from_left, 0)
        valid, d, copy = left_at(t)
        pass_on(valid, me == last, d, copy, from_right, 1)
        if t == 0:
            out[...] = made(me, 2)
        yield
    yield

    @pl.when(me > 0)
    def _():
        line.right(held.at[me], from_left.at[me], me).wait_recv()
        out[...] += from_left[me].astype(f32)

    @pl.when(me < last)
    def _():
        line.left(held.at[me], from_right.at[me], me).wait_recv()
        out[...] += from_right[me].astype(f32)

    for t in range(last):
        for valid, _, copy in (right_at(t), left_at(t)):
            pl.when(valid)(copy.wait_send)


def halves(rows):
    return [pl.ds(0, rows // 2), pl.ds(rows // 2, rows // 2)]


def gather_halves(axis, ref, size, send, recv):
    flows = []
    for h, at in enumerate(halves(ref.shape[0])):

        def slot_of(d, at=at):
            return ref.at[at, pl.ds(pl.multiple_of(d * size, size), size)]

        flows.append(line_gather(axis, slot_of, send.at[h], recv.at[h]))
    return flows


def scatter_halves(axis, block_of, out, held, from_left, from_right, send, recv):
    flows = []
    for h, at in enumerate(halves(out.shape[0])):
        flows.append(
            line_scatter(
                axis,
                functools.partial(block_of, at=at),
                out.at[at, :],
                held.at[:, at, :],
                from_left.at[:, at, :],
                from_right.at[:, at, :],
                send.at[h],
                recv.at[h],
            )
        )
    return flows


def run(*flows, pump=None):
    flows = list(flows)
    turn = 0
    while flows:
        flows = [flow for flow in flows if next(flow, flows) is not flows]
        if pump is not None and turn < len(pump[1]):
            pump[0].pump(pump[1][turn])
        turn += 1


def lanes(ref, size):
    return lambda d: ref.at[:, pl.ds(pl.multiple_of(d * size, size), size)]


def fetch(sources, targets, sems):
    copies = [pltpu.make_async_copy(s, t, sems.at[i]) for i, (s, t) in enumerate(zip(sources, targets))]
    for copy in copies:
        copy.start()
    return copies


def as_row(ref):
    return ref[...].reshape(1, ref.shape[0])


def lengths_row(lens):
    groups, per_group = lens.shape
    values = lens[...].astype(f32)
    at = lax.broadcasted_iota(jnp.int32, (per_group, groups * per_group), 1)
    inner = lax.broadcasted_iota(jnp.int32, (per_group, groups * per_group), 0)
    total = jnp.zeros((1, groups * per_group), f32)
    for g in range(groups):
        place = jnp.where(at == inner + g * per_group, 1.0, 0.0)
        total = total + jnp.dot(
            values[g : g + 1, :], place, precision=lax.Precision.HIGHEST, preferred_element_type=f32
        )
    return total


def spray(axis, src_of, dst, send, recv, base=0):
    copies = []
    for k in range(1, lax.axis_size(axis)):
        copy = remote(src_of(k), dst.at[k - 1], send.at[base + k - 1], recv.at[base + k - 1], away(axis, k))
        copy.start()
        copies.append(copy)
    return copies


def wait_all(copies):
    for copy in copies:
        copy.wait()


def swap(axis, src, dst, send, recv):
    copy = remote(src, dst, send, recv, away(axis, 1))
    copy.start()
    return copy


def sequence_rows(lens_row, order_row, per_group):
    count = lens_row.shape[1]
    ri = lax.broadcasted_iota(jnp.int32, (count, count), 0)
    ci = lax.broadcasted_iota(jnp.int32, (count, count), 1)
    lens_f = lens_row

    def to_column(row):
        return jnp.sum(jnp.where(ri == ci, row, 0.0), axis=1, keepdims=True)

    order_col = to_column(order_row.astype(f32)).astype(jnp.int32)
    lens_col = to_column(lens_f)
    pick = order_row == ri
    pick_t = order_col == ci
    slot_col = jnp.sum(jnp.where(pick_t, lens_f, 0.0), axis=1, keepdims=True)
    slot_row = jnp.sum(jnp.where(pick, lens_col, 0.0), axis=0, keepdims=True)
    start_col = jnp.sum(jnp.where(ci < ri, slot_row, 0.0), axis=1, keepdims=True)
    input_row = jnp.sum(jnp.where(pick_t, start_col, 0.0), axis=0, keepdims=True)
    same = (ri // per_group) == (ci // per_group)
    group_row = jnp.sum(jnp.where((ri < ci) & same, lens_col, 0.0), axis=0, keepdims=True)
    return lens_f, input_row, group_row


def place_rows(lens_row, order_row, per_group, group_rows, group):
    lens_f, input_row, group_row = sequence_rows(lens_row, order_row, per_group)
    count = lens_row.shape[1]
    rows = lax.broadcasted_iota(jnp.int32, (group_rows, count), 0).astype(f32)
    mine = (lax.broadcasted_iota(jnp.int32, (group_rows, count), 1) // per_group) == group
    inside = (rows >= group_row) & (rows < group_row + lens_f) & mine
    within = jnp.sum(jnp.where(inside, rows - group_row, 0.0), axis=1, keepdims=True)
    begin = jnp.sum(jnp.where(inside, input_row, 0.0), axis=1, keepdims=True)
    return begin + within, within


def owner_rows(lens_row, order_row, per_group, group_rows, block_rows, first):
    lens_f, input_row, group_row = sequence_rows(lens_row, order_row, per_group)
    count = lens_row.shape[1]
    rows = (lax.broadcasted_iota(jnp.int32, (block_rows, count), 0) + first).astype(f32)
    base = (lax.broadcasted_iota(jnp.int32, (block_rows, count), 1) // per_group) * group_rows
    inside = (rows >= input_row) & (rows < input_row + lens_f)
    found = jnp.where(inside, base.astype(f32) + group_row + rows - input_row, 0.0)
    return jnp.sum(found, axis=1, keepdims=True)


def plane_origin(rows, dp_size, col_size, block_rows):
    at = lax.broadcasted_iota(jnp.int32, (rows, dp_size * col_size * block_rows), 1)
    block = at // block_rows
    group = lax.rem(block, dp_size)
    column = block // dp_size
    return ((group * col_size + column) * block_rows + lax.rem(at, block_rows)).astype(f32)


def pick_rows(wanted, held):
    col_size, dp_size, block_rows, width = held.shape
    total = col_size * dp_size * block_rows
    chosen = wanted == plane_origin(wanted.shape[0], dp_size, col_size, block_rows)
    chosen = jnp.where(chosen, 1.0, 0.0).astype(bf16)
    return matmul(chosen, held.reshape(total, width)).astype(bf16)


def plane_start(src, held, send, recv):
    me, column = lax.axis_index("dp"), lax.axis_index("col")
    held[column, me] = src[...]
    copies = []
    for k in range(1, lax.axis_size("dp")):
        copy = remote(src, held.at[column, me], send.at[k], recv.at[k], away("dp", k))
        copy.start()
        copies.append(copy)
    return copies


def plane_swap(copies, held, send, recv):
    column = lax.axis_index("col")
    for copy in copies:
        copy.wait_recv()
    return swap("col", held.at[column], held.at[column], send.at[0], recv.at[0])


def plane_wait(copies, last):
    last.wait_recv()
    for copy in [*copies, last]:
        copy.wait_send()


def plane_finish(copies, held, send, recv):
    plane_wait(copies, plane_swap(copies, held, send, recv))


def total_of_sums(part, half_own, half_in, low_own, low_in, full, sems):
    send, recv = sems
    rows = part.shape[0] // 2
    column = lax.axis_index("col")
    mine = pl.ds(pl.multiple_of(column * rows, rows), rows)
    other = pl.ds(pl.multiple_of((1 - column) * rows, rows), rows)
    half_own[...] = part[other, :]
    copy = swap("col", half_own, half_in, send.at[0], recv.at[0])
    yield
    copy.wait()
    low_own[...] = (part[mine, :] + half_in[...]).astype(bf16)
    copies = spray("row", lambda k: low_own, low_in, send, recv, 1)
    yield
    wait_all(copies)
    total = low_own[...].astype(f32)
    for k in range(low_in.shape[0]):
        total = total + low_in[k].astype(f32)
    full[mine, :] = total
    copy = swap("col", full.at[mine], full.at[mine], send.at[4], recv.at[4])
    yield
    copy.wait()


def lanes_like(tile, width):
    if tile.shape[-1] == width:
        return tile
    return jnp.concatenate([tile] * (width // tile.shape[-1]), axis=-1)


def lane_mask(count, lanes, first):
    lane = lax.broadcasted_iota(jnp.int32, (count, lanes), 1)
    return lane == lax.broadcasted_iota(jnp.int32, (count, lanes), 0) + first


def spread(values, first, count, wide):
    rows, lanes = values.shape
    chosen = jnp.where(lane_mask(count, lanes, first)[None], values[:, None, :], 0.0)
    chosen = chosen.reshape(rows * count, lanes)
    high = chosen.astype(bf16)
    rest = (chosen - high.astype(f32)).astype(bf16)
    ones = jnp.ones((lanes, wide), bf16)
    return matmul(high, ones) + matmul(rest, ones)


def spread_into(target, source, start, first, count):
    rows, _, wide = target.shape
    size = min(32, rows)

    def one(j, _):
        at = pl.ds(pl.multiple_of(start + j * size, size), size)
        found = spread(source[at, :], first, count, wide)
        target[pl.ds(pl.multiple_of(j * size, size), size)] = found.reshape(size, count, wide)
        return 0

    lax.fori_loop(0, rows // size, one, 0)


def add_lane_sums(target, start, sources):
    rows = sources[0][0].shape[0]
    size = min(32, rows)

    def one(j, _):
        inner = pl.ds(pl.multiple_of(j * size, size), size)
        at = pl.ds(pl.multiple_of(start + j * size, size), size)
        total = target[at, :]
        for source, first in sources:
            total = total + lane_sums(source[inner], first, target.shape[1])
        target[at, :] = total
        return 0

    lax.fori_loop(0, rows // size, one, 0)


def lane_sums(values, first, lanes):
    rows, count, wide = values.shape
    flat = values.reshape(rows * count, wide)
    high = flat.astype(bf16)
    rest = (flat - high.astype(f32)).astype(bf16)
    ones = jnp.ones((wide, lanes), bf16)
    sums = (matmul(high, ones) + matmul(rest, ones)).reshape(rows, count, lanes)
    return jnp.sum(jnp.where(lane_mask(count, lanes, first)[None], sums, 0.0), axis=1)


def scan_forward(proj, b_at, c_at, gone_step, drive, rate, bb, cb, y):
    rows, width = drive.shape
    count = rate.shape[0]
    piece, _, wide = bb.shape
    state = jnp.zeros((count, width), f32)
    for start in range(0, rows, piece):
        spread_into(bb, proj, start, b_at, count)
        spread_into(cb, proj, start, c_at, count)

        def eight(k, state):
            inner = pl.multiple_of(k * 8, 8)
            base = pl.multiple_of(start + k * 8, 8)
            gone = gone_step[pl.ds(base, 8), :]
            driven = drive[pl.ds(base, 8), :]
            found = []
            for i in range(8):
                decay = jnp.exp(gone[i : i + 1, :] * rate)
                state = decay * state + driven[i : i + 1, :] * lanes_like(bb[inner + i], width)
                found.append(jnp.sum(state * lanes_like(cb[inner + i], width), axis=0, keepdims=True))
            y[pl.ds(base, 8), :] = jnp.concatenate(found, axis=0)
            return state

        state = lax.fori_loop(0, piece // 8, eight, state)
        yield


def scan_states(proj, b_at, gone_step, drive, rate, bb, hs):
    rows, width = drive.shape
    count = rate.shape[0]
    piece, _, wide = bb.shape
    hs[0] = jnp.zeros((count, width), f32)
    for start in range(0, rows, piece):
        spread_into(bb, proj, start, b_at, count)

        def eight(k, state):
            inner = pl.multiple_of(k * 8, 8)
            base = pl.multiple_of(start + k * 8, 8)
            gone = gone_step[pl.ds(base, 8), :]
            driven = drive[pl.ds(base, 8), :]
            for i in range(8):
                decay = jnp.exp(gone[i : i + 1, :] * rate)
                state = decay * state + driven[i : i + 1, :] * lanes_like(bb[inner + i], width)
                hs[base + i + 1] = state
            return state

        lax.fori_loop(0, piece // 8, eight, hs[start])
        yield


def scan_backward(
    proj, b_at, c_at, step, gone_step, drive, inner_u, dy, rate, hs, bb, cb, pb, pc, du, dstep, dproj
):
    rows, width = drive.shape
    count = rate.shape[0]
    piece, _, wide = bb.shape

    def fold(values):
        total = values[:, 0:wide]
        for j in range(1, width // wide):
            total = total + values[:, j * wide : (j + 1) * wide]
        return total

    def part(start, carry):
        spread_into(bb, proj, start, b_at, count)
        spread_into(cb, proj, start, c_at, count)

        def eight(k, carry):
            later, total = carry
            inner = pl.multiple_of((piece // 8 - 1 - k) * 8, 8)
            base = pl.multiple_of(start + inner, 8)
            step8 = step[pl.ds(base, 8), :]
            gone8 = gone_step[pl.ds(base, 8), :]
            drive8 = drive[pl.ds(base, 8), :]
            u8 = inner_u[pl.ds(base, 8), :]
            dy8 = dy[pl.ds(base, 8), :]
            by_b = [None] * 8
            by_rate = [None] * 8
            for i in reversed(range(8)):
                dy_row = dy8[i : i + 1, :]
                lam = lanes_like(cb[inner + i], width) * dy_row + later
                later = jnp.exp(gone8[i : i + 1, :] * rate) * lam
                kept = later * hs[base + i]
                total = total + kept * step8[i : i + 1, :]
                by_b[i] = jnp.sum(lam * lanes_like(bb[inner + i], width), axis=0, keepdims=True)
                by_rate[i] = jnp.sum(kept * rate, axis=0, keepdims=True)
                pb[inner + i] = fold(lam * drive8[i : i + 1, :])
                pc[inner + i] = fold(hs[base + i + 1] * dy_row)
            by_b = jnp.concatenate(by_b, axis=0)
            by_rate = jnp.concatenate(by_rate, axis=0)
            du[pl.ds(base, 8), :] = by_b * step8
            dstep[pl.ds(base, 8), :] = by_rate + by_b * u8
            return later, total

        carry = lax.fori_loop(0, piece // 8, eight, carry)
        add_lane_sums(dproj, start, ((pb, b_at), (pc, c_at)))
        return carry

    blank = jnp.zeros((count, width), f32)
    carry = (blank, blank)
    for start in reversed(range(0, rows, piece)):
        carry = part(start, carry)
        yield
    return carry[1] * rate


RANK_LANES = 128


def scan_kernel(proj, gone, drive, rate, y, bb, cb, *, b_at, c_at):
    run(scan_forward(proj, b_at, c_at, gone, drive, rate[...], bb, cb, y))


def adjoint_kernel(
    proj, step, gone, drive, inner_u, dy, rate, du, dstep, dproj, drate, bb, cb, hs, pb, pc, *, b_at, c_at
):
    run(scan_states(proj, b_at, gone, drive, rate[...], bb, hs))
    dproj[...] = jnp.zeros_like(dproj)
    kept = {}

    def adjoint():
        kept["rate"] = yield from scan_backward(
            proj, b_at, c_at, step, gone, drive, inner_u, dy, rate[...], hs, bb, cb, pb, pc, du, dstep, dproj
        )

    run(adjoint())
    drate[...] = kept["rate"]


def scan_sizes(rows, width, count):
    wide = 128 if width % 128 == 0 else width
    piece = min(128, rows)
    return pltpu.VMEM((piece, count, wide), f32)


def scan_alone(proj, gone, drive, rate, b_at, c_at):
    rows, width = drive.shape
    block = scan_sizes(rows, width, rate.shape[0])
    return pl.pallas_call(
        functools.partial(scan_kernel, b_at=b_at, c_at=c_at),
        out_shape=jax.ShapeDtypeStruct((rows, width), f32),
        scratch_shapes=[block, block],
        compiler_params=pltpu.CompilerParams(vmem_limit_bytes=VMEM_BYTES),
        name="scan_states",
    )(proj, gone, drive, rate)


def adjoint_alone(proj, step, gone, drive, inner_u, dy, rate, b_at, c_at):
    rows, width = step.shape
    count = rate.shape[0]
    block = scan_sizes(rows, width, count)
    shape = jax.ShapeDtypeStruct
    return pl.pallas_call(
        functools.partial(adjoint_kernel, b_at=b_at, c_at=c_at),
        out_shape=(
            shape((rows, width), f32),
            shape((rows, width), f32),
            shape(proj.shape, f32),
            shape((count, width), f32),
        ),
        scratch_shapes=[
            block,
            block,
            pltpu.VMEM((rows + 1, count, width), f32),
            block,
            block,
        ],
        compiler_params=pltpu.CompilerParams(vmem_limit_bytes=VMEM_BYTES),
        name="scan_adjoint",
    )(proj, step, gone, drive, inner_u, dy, rate)


PUMPS = ((0, 1, 1), (1, 0, 1), 0, (1, 2, 1), (1, 1), (0, 0, 0), (2, 2, 1), 0, 2)


def conv_sum(inner_x, place, taps, bias):
    count = taps.shape[0]
    total = bias + inner_x * taps[count - 1 : count, :]
    for shift in range(1, count):
        moved = jnp.where(place >= shift, pltpu.roll(inner_x, shift, 0), 0.0)
        total = total + moved * taps[count - 1 - shift : count - shift, :]
    return total


def transposed(left, right):
    return lax.dot_general(left, right, (((1,), (1,)), ((), ())), preferred_element_type=f32)


def over_rows(left, right):
    return lax.dot_general(left, right, (((0,), (0,)), ((), ())), preferred_element_type=f32)


def columns(d, size):
    return pl.ds(pl.multiple_of(d * size, size), size)


def line_total(own, arrived):
    total = own
    for k in range(arrived.shape[0]):
        total = total + arrived[k]
    return total


def forward_kernel(
    x, cot, lens, order, gain1, taps, bias, w_xp, w_dt, dt_bias, a_log, skip, gain2,
    w_x_h, w_z_h, w_out_h, w_gate_h, w_up_h, w_down_h,
    xg_o, cg_o, n1_o, s1_o, place_o, xi_o, z_o, proj_o, yv_o, go_all, h1_o, s2_o, n2_o, hid_all, dgu_o, dot_o, n1_mates, n2_mates, cg_mates, go_mates, hid_mates,
    w_x, w_z, w_out, w_gate, w_up, w_down, w_step, rate,
    x_all, c_all, sum_own, sum_in, low, xi_held, xi_left, xi_right, z_held, z_left, z_right,
    part_s, half_own, half_in, low_own, low_in, bb, cb, step, gone, drive,
    own, other, gu, gu_part, gu_held, gu_left, gu_right, dhid, h_held, h_left, h_right,
    w_sems, x_send, x_recv, c_send, c_recv, sum_send, sum_recv, xi_send, xi_recv, z_send, z_recv, t_send, t_recv,
    go_send, go_recv, o_send, o_recv, sum2_send, sum2_recv, gu_send, gu_recv, h_send, h_recv, hid_send, hid_recv, m_send, m_recv,
    *, model_width, rank, count, leave
):
    rows, width = xi_o.shape
    hidden = dgu_o.shape[1] // 2
    group, row = lax.axis_index("dp"), lax.axis_index("row")
    row_size = lax.axis_size("row")
    weights = fetch(
        (w_x_h, w_z_h, w_out_h, w_gate_h, w_up_h, w_down_h), (w_x, w_z, w_out, w_gate, w_up, w_down), w_sems
    )
    met = greet("dp", "row", "col")
    w_step[...] = jnp.zeros_like(w_step)
    w_step[0:rank, :] = w_dt[...]
    met()
    x_copies = plane_start(x, x_all, x_send, x_recv)
    lens_row = lengths_row(lens)
    source, place = place_rows(lens_row, as_row(order), lens.shape[1], rows, group)
    place_o[...] = place
    plane_finish(x_copies, x_all, x_send, x_recv)
    c_copies = plane_start(cot, c_all, c_send, c_recv)
    xg_low = pick_rows(source, x_all[...])
    xg_o[...] = xg_low
    xg = xg_low.astype(f32)
    gain1_now = as_row(gain1)
    low[...] = (xg * gain1_now).astype(bf16)
    weights[0].wait()
    kept = {}

    def during_xi():
        sum_own[...] = rows_form(xg * xg)
        sum_copies = spray("row", lambda k: sum_own, sum_in, sum_send, sum_recv)
        rate[...] = -jnp.exp(a_log[...])
        yield
        wait_all(sum_copies)
        kept["s1"] = column_form(lax.rsqrt(line_total(sum_own[...], sum_in) / model_width + epsilon))
        s1_o[...] = kept["s1"]
        leave("xg", "s1", "place")
        kept["cot"] = plane_swap(c_copies, c_all, c_send, c_recv)

    run(
        *scatter_halves(
            "row", lambda d, at: matmul(low[at, :], w_x[:, columns(d, width)]), xi_o, xi_held, xi_left, xi_right,
            xi_send, xi_recv,
        ),
        during_xi(),
    )
    weights[1].wait()
    z_flows = scatter_halves(
        "row", lambda d, at: matmul(low[at, :], w_z[:, columns(d, width)]), z_o, z_held, z_left, z_right, z_send, z_recv
    )
    for flow in z_flows:
        next(flow)
    s1 = kept["s1"]
    inner_x = xi_o[...] * s1
    xi_o[...] = inner_x
    u_low = silu(conv_sum(inner_x, place, taps[...], as_row(bias))).astype(bf16)
    u = u_low.astype(f32)
    part_s[...] = matmul(u_low, w_xp[...])

    def mix():
        yield from total_of_sums(part_s, half_own, half_in, low_own, low_in, proj_o, (t_send, t_recv))
        pre = matmul(proj_o[...].astype(bf16), w_step[...]) + as_row(dt_bias)
        step_now = jax.nn.softplus(pre)
        step[...] = step_now
        gone[...] = jnp.where(place > 0.0, step_now, 1e30)
        drive[...] = step_now * u
        yield from scan_forward(proj_o, rank, rank + count, gone, drive, rate[...], bb, cb, yv_o)

    mixing = mix()
    next(mixing)
    plane_wait(c_copies, kept["cot"])
    cg_o[...] = pick_rows(source, c_all[...])
    kept["mates"] = to_mates(cg_o, cg_mates, m_send.at[1], m_recv.at[1])
    next(mixing)
    run(*z_flows, mixing)
    yv = yv_o[...] + as_row(skip) * u
    yv_o[...] = yv
    z = z_o[...] * s1
    z_o[...] = z
    go_all[:, columns(row, width)] = (yv * silu(z)).astype(bf16)

    def during_gather():
        n1_o[...] = (xg * s1 * gain1_now).astype(bf16)
        kept["mates"] += to_mates(n1_o, n1_mates, m_send.at[0], m_recv.at[0])
        yield

    weights[5].wait()
    run(
        *gather_halves("row", go_all, width, go_send, go_recv),
        *scatter_halves(
            "row", lambda d, at: transposed(cg_o[at, :], w_down[columns(d, hidden), :]), dhid, h_held, h_left, h_right,
            h_send, h_recv,
        ),
        during_gather(),
    )
    kept["mates"] += quarters_to_mates(go_all, go_mates, m_send.at[3], m_recv.at[3])
    weights[2].wait()
    own[...] = matmul(go_all[...], w_out[...])
    copy = swap("col", own, other, o_send.at[0], o_recv.at[0])
    weights[3].wait()
    weights[4].wait()
    copy.wait()
    h1 = xg + (own[...] + other[...])
    h1_o[...] = h1
    gain2_now = as_row(gain2)
    low[...] = (h1 * gain2_now).astype(bf16)

    def gate_up_flows(first):
        rows_now, size = rows // 2, rows // 4

        def block_of(d, slot, part):
            side = columns(d, hidden)
            if part == 0:
                left = low[first : first + rows_now, :]
                gu_part[slot, :, 0:hidden] = matmul(left, w_gate[:, side])
                gu_part[slot, :, hidden:] = matmul(left, w_up[:, side])
            return gu_part[slot, part * size : (part + 1) * size, :]

        flows = []
        for part in range(2):
            at = pl.ds(first + part * size, size)
            number = first // size + part
            flows.append(
                line_scatter(
                    "row", functools.partial(block_of, part=part), gu.at[at, :], gu_held.at[:, at, :],
                    gu_left.at[:, at, :], gu_right.at[:, at, :], gu_send.at[number], gu_recv.at[number], slots=True,
                )
            )
        return flows

    def hid_flows(first, count):
        size = rows // 2 // count
        flows = []
        for part in range(count):
            at = pl.ds(first + part * size, size)

            def slot_of(d, at=at):
                return hid_all.at[at, columns(d, hidden)]

            number = first // (rows // 4) + part
            flows.append(line_gather("row", slot_of, hid_send.at[number], hid_recv.at[number]))
        return flows

    def activate(first):
        at = slice(first, first + rows // 2)
        s2 = s2_o[at, :]
        gate, up = gu[at, 0:hidden] * s2, gu[at, hidden:] * s2
        gu[at, 0:hidden], gu[at, hidden:] = gate, up
        sig = jax.nn.sigmoid(gate)
        act = gate * sig
        hid_all[at, columns(row, hidden)] = (act * up).astype(bf16)
        d_hid = dhid[at, :]
        dgu_o[at, 0:hidden] = (d_hid * up * (sig * (1.0 + gate * (1.0 - sig)))).astype(bf16)
        dgu_o[at, hidden:] = (d_hid * act).astype(bf16)

    def during_scatter():
        sum_own[...] = rows_form(h1 * h1)
        sum_copies = spray("row", lambda k: sum_own, sum_in, sum2_send, sum2_recv)
        yield
        wait_all(sum_copies)
        s2 = column_form(lax.rsqrt(line_total(sum_own[...], sum_in) / model_width + epsilon))
        s2_o[...] = s2
        n2_o[...] = (h1 * s2 * gain2_now).astype(bf16)
        leave("n1", "cg", "xi", "z", "proj", "yv", "go_all", "h1", "s2", "n2")
        kept["mates"] += to_mates(n2_o, n2_mates, m_send.at[2], m_recv.at[2])

    def dots():
        yield
        dot_o[...] = rows_form(dgu_o[...].astype(f32) * gu[...])

    run(*gate_up_flows(0), during_scatter())
    activate(0)
    run(*gate_up_flows(rows // 2), *hid_flows(0, 1))
    activate(rows // 2)
    top, bottom = pl.ds(0, rows // 2), pl.ds(rows // 2, rows // 2)
    kept["mates"] += quarters_to_mates(hid_all, hid_mates, m_send.at[4], m_recv.at[4], top)
    run(*hid_flows(rows // 2, 2), dots())
    kept["mates"] += quarters_to_mates(hid_all, hid_mates, m_send.at[5], m_recv.at[5], bottom)
    leave("hid_all", "dgu", "dot")
    wait_all(kept["mates"])
    leave("hid_mates", "n1_mates", "n2_mates", "cg_mates", "go_mates")
    leave.finish()


def dp_bits():
    me = lax.axis_index("dp")
    return lax.rem(me, 2), me // 2


def dp_mates():
    me = lax.axis_index("dp")
    along_x, along_y = dp_bits()
    return {"dp": me + 1 - 2 * along_x}, {"dp": me + 2 - 4 * along_y}


def to_mates(src, dst, send, recv):
    copies = [remote(src, dst.at[h], send.at[h], recv.at[h], mate) for h, mate in enumerate(dp_mates())]
    for copy in copies:
        copy.start()
    return copies


def quarters_to_mates(ref, dst, send, recv, rows=None):
    size = ref.shape[1] // 4
    at = pl.ds(0, ref.shape[0]) if rows is None else rows
    copies = []
    for h, (near, mate) in enumerate(zip(dp_bits(), dp_mates())):
        side = pl.ds(pl.multiple_of((2 * h + 1 - near) * size, size), size)
        copies.append(remote(ref.at[at, side], dst.at[h, at, :], send.at[h], recv.at[h], mate))
        copies[-1].start()
    return copies


def pair_sum(grad, sent, fixed, fixed_mates, by_rows, sent_in, second_in, third_in, send, recv, swapped="sent"):
    quarter = sent.shape[1] // 4
    eighth = (quarter if by_rows else grad.shape[0]) // 2
    bits, mates = dp_bits(), dp_mates()

    def side(h, near):
        return pl.ds(pl.multiple_of((2 * h + near) * quarter, quarter), quarter)

    def view(h, near, far):
        if by_rows:
            return grad.at[pl.ds(pl.multiple_of((2 * h + near) * quarter + far * eighth, eighth), eighth), :]
        return grad.at[pl.ds(pl.multiple_of(far * eighth, eighth), eighth), side(h, near)]

    class Half:
        def __init__(self, h):
            near, far = bits[h], bits[1 - h]
            mate, other = mates[h], mates[1 - h]

            def copy(stage, src, dst, to):
                return remote(src, dst, send.at[stage, h], recv.at[stage, h], to)

            self.h, self.near = h, near
            self.own, self.rest = view(h, near, far), view(h, near, 1 - far)
            there = view(h, 1 - near, far), view(h, 1 - near, 1 - far)
            first = None
            if swapped == "fixed":
                first = copy(0, fixed, fixed_mates.at[h], mate)
            elif swapped == "sent":
                first = copy(0, sent.at[:, side(h, 1 - near)], sent_in.at[h], mate)
            self.out = (
                first,
                copy(1, self.rest, second_in.at[h], other),
                copy(2, self.own, third_in.at[h], other),
                copy(3, self.own, self.own, mate),
                copy(4, self.rest, self.rest, mate),
            )
            self.back = (copy(3, there[0], there[0], mate), copy(4, there[1], there[1], mate))

        def product(self):
            mine, mates_part = sent[:, side(self.h, self.near)], sent_in[self.h]
            if by_rows:
                found = over_rows(mine, fixed[...]) + over_rows(mates_part, fixed_mates[self.h])
                grad[side(self.h, self.near), :] = found.astype(bf16)
            else:
                found = over_rows(fixed[...], mine) + over_rows(fixed_mates[self.h], mates_part)
                grad[:, side(self.h, self.near)] = found.astype(bf16)

    both_halves = (Half(0), Half(1))
    if swapped:
        for half in both_halves:
            half.out[0].start()
        yield
    for half in both_halves:
        if swapped:
            half.out[0].wait_recv()
        half.product()
        half.out[1].start()
    yield
    for half in both_halves:
        half.out[1].wait_recv()
        add_view(half.own, second_in.at[half.h], eighth)
        half.out[2].start()
        half.out[3].start()
    yield
    for half in both_halves:
        half.out[2].wait_recv()
        half.out[1].wait_send()
        half.rest[...] = third_in[half.h]
        half.out[4].start()
    yield
    for half in both_halves:
        for copy in half.back:
            copy.wait_recv()
        for stage in (0, 2, 3, 4) if swapped else (2, 3, 4):
            half.out[stage].wait_send()


def add_view(target, source, rows):
    def piece(j, _):
        at = pl.ds(pl.multiple_of(j * 16, 16), 16)
        target[at, :] = (target[at, :].astype(f32) + source[at, :].astype(f32)).astype(bf16)
        return 0

    lax.fori_loop(0, rows // 16, piece, 0)


def add_rows(target, base, source, rows):
    def piece(j, _):
        at = pl.ds(pl.multiple_of(base + j * 16, 16), 16)
        found = target[at, :].astype(f32) + source[pl.ds(pl.multiple_of(j * 16, 16), 16), :].astype(f32)
        target[at, :] = found.astype(target.dtype)
        return 0

    lax.fori_loop(0, rows // 16, piece, 0)


def plane_sum(grad, first_in, second_in, send, recv, free):
    quarter = grad.shape[0] // 4
    eighth = quarter // 2
    bits, partners = dp_bits(), dp_mates()

    def rows(ref, start, count):
        return ref.at[pl.ds(pl.multiple_of(start, 16), count), :]

    class Half:
        def __init__(self, h):
            near, far = bits[h], bits[1 - h]
            self.free, self.mate, self.first = free.at[h], partners[h], first_in.at[h]
            base = h * 2 * quarter
            self.kept = base + near * quarter
            self.own = self.kept + far * eighth
            self.rest = self.kept + (1 - far) * eighth
            self.rest_in = (1 - far) * eighth
            across = base + (1 - near) * quarter
            self.second = second_in.at[h]

            def copy(stage, src, dst, to):
                return remote(src, dst, send.at[stage, h], recv.at[stage, h], to)

            mate, other = partners[h], partners[1 - h]
            own, rest = rows(grad, self.own, eighth), rows(grad, self.rest, eighth)
            there = (rows(grad, across + far * eighth, eighth), rows(grad, across + (1 - far) * eighth, eighth))
            back = rows(self.first, self.rest_in, eighth)
            self.out = (
                copy(0, rows(grad, across, quarter), self.first, mate),
                copy(1, rest, self.second, other),
                copy(2, own, rows(self.first, far * eighth, eighth), other),
                copy(3, own, own, mate),
                copy(4, rest, rest, mate),
            )
            self.back = (
                None,
                None,
                copy(2, back, back, other),
                copy(3, there[0], there[0], mate),
                copy(4, there[1], there[1], mate),
            )

    halves = (Half(0), Half(1))
    for half in halves:
        half.out[0].start()
    yield
    for half in halves:
        half.out[0].wait_recv()
        add_rows(grad, half.kept, half.first, quarter)
        half.out[1].start()
        half.out[0].wait_send()
        pl.semaphore_signal(half.free, inc=1, device_id=half.mate, device_id_type=MESH)
    yield
    for half in halves:
        half.out[1].wait_recv()
        add_rows(grad, half.own, half.second, eighth)
        half.out[2].start()
        pl.semaphore_wait(half.free, 1)
        half.out[3].start()
    yield
    for half in halves:
        half.back[2].wait_recv()
        half.out[1].wait_send()
        grad[pl.ds(pl.multiple_of(half.rest, 16), eighth), :] = half.first[
            pl.ds(pl.multiple_of(half.rest_in, 16), eighth), :
        ]
        half.out[4].start()
    yield
    for half in halves:
        half.back[3].wait_recv()
        half.back[4].wait_recv()
        for copy in half.out[2:]:
            copy.wait_send()


class Sums:
    def __init__(self):
        self.active = []

    def add(self, flow):
        next(flow)
        self.active.append(flow)

    def pump(self, count=1):
        for _ in range(count):
            if self.active:
                flow = self.active.pop(0)
                if next(flow, self) is not self:
                    self.active.append(flow)

    def drain(self):
        while self.active:
            self.pump()


def backward_kernel(
    lens, order, gain2, taps, bias, w_xp, w_dt, dt_bias, a_log, skip, gain1,
    w_gate_h, w_up_h, w_down_h, w_out_h, w_x_h, w_z_h,
    y_o, dx_o, small_o, g_down_o, g_gate_o, g_up_o, g_z_o, g_x_o, g_out_o,
    w_gate, w_up, w_down, w_out, w_x, w_z, w_step, rate,
    dg_all, du_all, dz_all, dxi_all, dh1, dmix, y_own, dx_own, y_all, dx_all,
    own, other, y_part, y_other, dot_in, dot_own, dot_sum, dot_other,
    dgo, d_held, d_left, d_right,
    hs, bb, cb, pb, pc, step, gone, drive, u_s, dy_s, du_s, dstep, dproj,
    half_own, half_in, low_own, low_in, full,
    g_down, g_gate, g_up, g_z, g_x, g_out, small,
    g_gate_1, g_up_1, g_z_1, g_x_1, small_1,
    g_down_2, g_gate_2, g_up_2, g_z_2, g_x_2, g_out_2, small_2,
    g_down_3, g_gate_3, g_up_3, g_z_3, g_x_3, g_out_3, dmix_mates,
    w_sems, g_send, g_recv, u_send, u_recv, o_send, o_recv, dot_send, dot_recv,
    y_send, y_recv, dx_send, dx_recv, d_send, d_recv, z_send, z_recv, t_send, t_recv, x_send, x_recv,
    dot2_send, dot2_recv, sum_send, sum_recv, sum_free, write_sems,
    *, rank, model_width, late
):
    rows, width = dgo.shape
    count = rate.shape[0]
    block = y_o.shape[0]
    tap_count = taps.shape[0]
    group, row, column = lax.axis_index("dp"), lax.axis_index("row"), lax.axis_index("col")
    row_size, col_size = lax.axis_size("row"), lax.axis_size("col")
    weights = fetch(
        (w_down_h, w_gate_h, w_up_h, w_out_h, w_x_h, w_z_h), (w_down, w_gate, w_up, w_out, w_x, w_z), w_sems
    )
    half = columns(column, block)
    sums = Sums()
    writes = []

    def write(number, grad, result):
        copy = pltpu.make_async_copy(grad, result, write_sems.at[number])
        copy.start()
        writes.append(copy)

    def total(number, grad, first_in, second_in, result):
        yield from plane_sum(
            grad, first_in, second_in, sum_send.at[number], sum_recv.at[number], sum_free.at[number]
        )
        write(number, grad, result)

    def pair(number, grad, sent, fixed, fixed_mates, by_rows, ins, result, swapped="sent"):
        yield from pair_sum(
            grad, sent, fixed, fixed_mates, by_rows, *ins, sum_send.at[number], sum_recv.at[number], swapped
        )
        write(number, grad, result)

    met = greet("dp", "row", "col")
    dgu = late("dgu")
    hidden = dgu.shape[1] // 2
    dg_all[:, columns(row, hidden)] = dgu[:, 0:hidden]
    du_all[:, columns(row, hidden)] = dgu[:, hidden:]
    dot, hid_all, cg, cg_mates = late("dot"), late("hid_all"), late("cg"), late("cg_mates")
    hid_mates = late("hid_mates")
    met()
    dot_copies = spray("row", lambda k: dot, dot_in, dot_send, dot_recv)

    def first_work():
        sums.add(pair(0, g_down, hid_all, cg, cg_mates, True, (hid_mates, g_down_2, g_down_3), g_down_o, None))
        yield
        weights[0].wait()
        y_part[...] = matmul(hid_all[...], w_down[...])
        y_copy = swap("col", y_part, y_other, o_send.at[0], o_recv.at[0])
        yield
        wait_all(dot_copies)
        dot_own[...] = line_total(dot[...], dot_in)
        dot_copy = swap("col", dot_own, dot_other, o_send.at[2], o_recv.at[2])
        weights[1].wait()
        weights[2].wait()
        yield
        y_copy.wait()
        dot_copy.wait()
        y_own[...] = (late("h1")[...] + (y_part[...] + y_other[...])).astype(bf16)

    run(*gather_halves("row", dg_all, hidden, g_send, g_recv), first_work(), pump=(sums, PUMPS[0]))
    n2, n2_mates = late("n2"), late("n2_mates")
    sums.add(pair(1, g_gate, dg_all, n2, n2_mates, False, (g_gate_1, g_gate_2, g_gate_3), g_gate_o))

    def second_work():
        own[...] = transposed(dg_all[...], w_gate[...])
        yield

    run(*gather_halves("row", du_all, hidden, u_send, u_recv), second_work(), pump=(sums, PUMPS[1]))
    own[...] += transposed(du_all[...], w_up[...])
    copy = swap("col", own, other, o_send.at[1], o_recv.at[1])
    sums.add(pair(2, g_up, du_all, n2, n2_mates, False, (g_up_1, g_up_2, g_up_3), g_up_o))
    sums.pump(PUMPS[2])
    copy.wait()
    h1_now, s2_now = late("h1")[...], late("s2")[...]
    dn2 = own[...] + other[...]
    dots = column_form(dot_own[...] + dot_other[...])
    dh1_now = (
        cg[...].astype(f32)
        + s2_now * (as_row(gain2) * dn2)
        - h1_now * (s2_now * s2_now * dots / model_width)
    )
    dh1[...] = dh1_now
    dmix[...] = dh1_now.astype(bf16)
    gnorm2 = jnp.sum(dn2 * h1_now * s2_now, axis=0, keepdims=True)

    inner_x = late("xi")[...]
    place_now = late("place")[...]
    proj = late("proj")
    kept = {}

    def states():
        go_all = late("go_all")
        sums.add(
            pair(5, g_out, go_all, dmix, dmix_mates, True, (late("go_mates"), g_out_2, g_out_3), g_out_o, "fixed")
        )
        w_step[...] = jnp.zeros_like(w_step)
        w_step[0:rank, :] = w_dt[...]
        rate[...] = -jnp.exp(a_log[...])
        xc = conv_sum(inner_x, place_now, taps[...], as_row(bias))
        sig_c = jax.nn.sigmoid(xc)
        u_low = (xc * sig_c).astype(bf16)
        u = u_low.astype(f32)
        u_s[...] = u
        step_low = proj[...].astype(bf16)
        pre = matmul(step_low, w_step[...]) + as_row(dt_bias)
        step_now = jax.nn.softplus(pre)
        step[...] = step_now
        gone[...] = jnp.where(place_now > 0.0, step_now, 1e30)
        drive[...] = step_now * u
        kept.update(xc=xc, sig_c=sig_c, u_low=u_low, u=u, step_low=step_low, pre=pre)
        yield from scan_states(proj, rank, gone, drive, rate[...], bb, hs)

    weights[3].wait()
    run(
        *scatter_halves(
            "row", lambda d, at: transposed(dmix[at, :], w_out[columns(d, width), :]), dgo, d_held, d_left, d_right,
            d_send, d_recv,
        ),
        states(),
        pump=(sums, PUMPS[3]),
    )
    xc, sig_c, u_low, u = kept["xc"], kept["sig_c"], kept["u_low"], kept["u"]
    step_low, pre = kept["step_low"], kept["pre"]
    z_now = late("z")[...]
    sig_z = jax.nn.sigmoid(z_now)
    d_z = (dgo[...] * late("yv")[...] * (sig_z * (1.0 + z_now * (1.0 - sig_z)))).astype(bf16)
    mine = dz_all.at[:, columns(row, width)]
    mine[...] = d_z
    z_copies = []
    for k in range(1, row_size):
        copy = remote(mine, mine, z_send.at[k - 1], z_recv.at[k - 1], away("row", k))
        copy.start()
        z_copies.append(copy)
    dy = dgo[...] * (z_now * sig_z)
    dy_s[...] = dy
    dproj[...] = jnp.zeros_like(dproj)

    def adjoint():
        kept["rate"] = yield from scan_backward(
            proj, rank, rank + count, step, gone, drive, u_s, dy_s, rate[...], hs, bb, cb, pb, pc, du_s, dstep, dproj
        )

    run(adjoint(), pump=(sums, PUMPS[4]))
    g_rate = kept["rate"]
    d_pre = dstep[...] * jax.nn.sigmoid(pre)
    d_pre_low = d_pre.astype(bf16)
    dproj[...] += transposed(d_pre_low, w_step[...])

    def during_sums():
        yield
        wait_all(z_copies)
        sums.add(pair(3, g_z, dz_all, late("n1"), late("n1_mates"), False, (g_z_1, g_z_2, g_z_3), g_z_o))

    run(
        total_of_sums(dproj, half_own, half_in, low_own, low_in, full, (t_send, t_recv)),
        during_sums(),
        pump=(sums, PUMPS[5]),
    )
    dproj_low = full[...].astype(bf16)
    du = du_s[...] + as_row(skip) * dy + transposed(dproj_low, w_xp[...])
    dxc = du * (sig_c * (1.0 + xc * (1.0 - sig_c)))
    taps_now = taps[...]
    d_inner = dxc * taps_now[tap_count - 1 : tap_count, :]
    masked = [dxc]
    for shift in range(1, tap_count):
        masked.append(jnp.where(place_now >= shift, dxc, 0.0))
        k = tap_count - 1 - shift
        d_inner = d_inner + pltpu.roll(masked[shift], rows - shift, 0) * taps_now[k : k + 1, :]
    d_inner = d_inner.astype(bf16)
    dxi_all[:, columns(row, width)] = d_inner

    def during():
        dot_own[...] = rows_form(d_inner.astype(f32) * inner_x + d_z.astype(f32) * z_now)
        dot_copies = spray("row", lambda k: dot_own, dot_in, dot2_send, dot2_recv)
        small[0:RANK_LANES, :] = over_rows(dproj_low, u_low).astype(bf16)
        small[RANK_LANES : RANK_LANES + rank, :] = over_rows(step_low, d_pre_low)[0:rank, :].astype(bf16)
        yield
        wait_all(dot_copies)
        dot_sum[...] = line_total(dot_own[...], dot_in)
        dot_copy = swap("col", dot_sum, dot_other, o_send.at[3], o_recv.at[3])
        weights[4].wait()
        weights[5].wait()
        own[...] = transposed(dz_all[...], w_z[...])
        yield
        dot_copy.wait()

    run(*gather_halves("row", dxi_all, width, x_send, x_recv), during(), pump=(sums, PUMPS[6]))
    own[...] += transposed(dxi_all[...], w_x[...])
    copy = swap("col", own, other, o_send.at[4], o_recv.at[4])
    sums.add(pair(4, g_x, dxi_all, late("n1"), late("n1_mates"), False, (g_x_1, g_x_2, g_x_3), g_x_o))
    sums.pump(PUMPS[7])
    copy.wait()
    dn1 = own[...] + other[...]
    s1_now = late("s1")[...]
    xg_now = late("xg")[...].astype(f32)
    dots = column_form(dot_sum[...] + dot_other[...])
    dx = dh1[...] + s1_now * (as_row(gain1) * dn1) - xg_now * (s1_now * s1_now * dots / model_width)
    dx_own[...] = dx.astype(bf16)
    dx_copies = plane_start(dx_own.at[half], dx_all, dx_send, dx_recv)
    y_copies = plane_start(y_own.at[half], y_all, y_send, y_recv)
    g_taps = [None] * tap_count
    for shift in range(tap_count):
        moved = pltpu.roll(inner_x, shift, 0) if shift else inner_x
        g_taps[tap_count - 1 - shift] = jnp.sum(masked[shift] * moved, axis=0, keepdims=True)
    pieces = [
        g_rate,
        *g_taps,
        jnp.sum(dxc, axis=0, keepdims=True),
        jnp.sum(d_pre, axis=0, keepdims=True),
        jnp.sum(dy * u, axis=0, keepdims=True),
        jnp.sum(dn1 * xg_now * s1_now, axis=0, keepdims=True),
        gnorm2,
    ]
    found = sum(piece.shape[0] for piece in pieces)
    pieces.append(jnp.zeros((small.shape[0] - RANK_LANES - rank - found, width), f32))
    small[RANK_LANES + rank :, :] = jnp.concatenate(pieces, axis=0).astype(bf16)
    sums.add(total(6, small, small_1, small_2, small_o))
    first = (group * col_size + column) * block
    wanted = owner_rows(lengths_row(lens), as_row(order), lens.shape[1], rows, block, first)
    sums.pump(PUMPS[8])
    plane_finish(dx_copies, dx_all, dx_send, dx_recv)
    dx_o[...] = pick_rows(wanted, dx_all[...])
    plane_finish(y_copies, y_all, y_send, y_recv)
    y_o[...] = pick_rows(wanted, y_all[...])
    sums.drain()
    for write in writes:
        write.wait()


def finish_kernel(
    y, dx, small, down, gate, up, z, x, out,
    y_o, dx_o, norm1_o, z_o, x_o, taps_o, bias_o, w_xp_o, w_dt_o, dt_bias_o, rate_o, skip_o, out_o, norm2_o, gate_o,
    up_o, down_o,
    *, rank
):
    for source, target in ((z, z_o), (x, x_o), (out, out_o), (gate, gate_o), (up, up_o), (down, down_o)):
        target[...] = source[...].astype(f32)

    @pl.when(pl.program_id(0) == 0)
    def _():
        y_o[...] = y[...]
        dx_o[...] = dx[...]
        values = small[...].astype(f32)
        w_xp_o[...] = jnp.transpose(values[0:RANK_LANES, :])
        w_dt_o[...] = values[RANK_LANES : RANK_LANES + rank, :]
        at = RANK_LANES + rank
        for target in (rate_o, taps_o):
            target[...] = values[at : at + target.shape[0], :]
            at += target.shape[0]
        for target in (bias_o, dt_bias_o, skip_o, norm1_o, norm2_o):
            target[...] = values[at : at + 1, :].reshape(target.shape)
            at += 1


VMEM_BYTES = 60 << 20
DMA = pltpu.SemaphoreType.DMA


def in_vmem(kernel, name, ident, outs, scratch, args, far=(), far_outs=(), late=None, leave=None):
    late, leave = late or {}, leave or {}
    space = pl.BlockSpec(memory_space=pltpu.VMEM)
    anywhere = pl.BlockSpec(memory_space=pl.ANY)
    heads, tails, before, after = len(args) + len(far), len(outs) + len(far_outs), len(late), len(leave)

    def whole(*refs):
        at = [0]

        def take(count):
            at[0] += count
            return refs[at[0] - count : at[0]]

        head, sources, tail, targets = take(heads), take(before), take(tails), take(after)
        middle = take(len(scratch))
        keywords = {}
        if late:
            held = take(before)
            keywords["late"] = Late(list(late), sources, held, take(1)[0])
        held = take(after)
        if leave:
            keywords["leave"] = Leave(list(leave), held, targets, take(1)[0])
        kernel(*head, *tail, *held, *middle, **keywords)

    own = list(scratch)
    if late:
        own += [pltpu.VMEM(value.shape, value.dtype) for value in late.values()] + [DMA((before,))]
    if leave:
        own += [pltpu.VMEM(shape, kind) for shape, kind in leave.values()] + [DMA((after,))]
    return pl.pallas_call(
        whole,
        out_shape=tuple(jax.ShapeDtypeStruct(shape, kind) for shape, kind in [*outs, *far_outs, *leave.values()]),
        in_specs=[space] * len(args) + [anywhere] * (len(far) + before),
        out_specs=tuple([space] * len(outs) + [anywhere] * (len(far_outs) + after)),
        scratch_shapes=own,
        compiler_params=pltpu.CompilerParams(
            collective_id=ident, has_side_effects=ident is not None, vmem_limit_bytes=VMEM_BYTES
        ),
        name=name,
    )(*args, *far, *late.values())


def both(*shape):
    return [DMA(shape), DMA(shape)]


def on_pairs(
    x_in, lengths, seq_order, norm1_gain, w_in_x, w_in_z, conv_w, conv_b, w_xp, w_dt, dt_bias, a_log,
    skip_weight, w_out, norm2_gain, w_gate, w_up, w_down, cotangent,
):
    dp, rs = lax.axis_size("dp"), lax.axis_size("row")
    block, wide_d = x_in.shape
    rows = block * 2
    model_width = wide_d * rs
    width = conv_w.shape[0]
    hidden = w_gate.shape[1] // rs
    rank, count, taps = w_dt.shape[0], a_log.shape[1], conv_w.shape[1]
    conv_taps = conv_w.T
    rates = a_log.T
    vm = pltpu.VMEM
    tile = vm((128, count, 128), f32)
    big = vm((rows, width), f32)
    model = vm((rows, wide_d), f32)
    sums = [vm((8, rows), f32), vm((rs - 1, 8, rows), f32)]
    sums_scratch = [
        vm((rows // 2, RANK_LANES), f32),
        vm((rows // 2, RANK_LANES), f32),
        vm((rows // 2, RANK_LANES), bf16),
        vm((rs - 1, rows // 2, RANK_LANES), bf16),
    ]

    def weight(value):
        return vm(value.shape, value.dtype)

    def line(size, width):
        return [vm((size, rows, width), bf16)] * 3

    leave = {
        "xg": ((rows, wide_d), bf16), "cg": ((rows, wide_d), bf16), "n1": ((rows, wide_d), bf16),
        "s1": ((rows, 1), f32), "place": ((rows, 1), f32), "xi": ((rows, width), f32), "z": ((rows, width), f32),
        "proj": ((rows, RANK_LANES), f32), "yv": ((rows, width), f32), "go_all": ((rows, rs * width), bf16),
        "h1": ((rows, wide_d), f32), "s2": ((rows, 1), f32), "n2": ((rows, wide_d), bf16),
        "hid_all": ((rows, rs * hidden), bf16), "dgu": ((rows, 2 * hidden), bf16), "dot": ((8, rows), f32),
        "n1_mates": ((2, rows, wide_d), bf16), "n2_mates": ((2, rows, wide_d), bf16),
        "cg_mates": ((2, rows, wide_d), bf16), "go_mates": ((2, rows, width), bf16),
        "hid_mates": ((2, rows, hidden), bf16),
    }
    passed = in_vmem(
        functools.partial(forward_kernel, model_width=model_width, rank=rank, count=count),
        "forward",
        0,
        [],
        [
            weight(w_in_x), weight(w_in_z), weight(w_out), weight(w_gate), weight(w_up), weight(w_down),
            vm((RANK_LANES, width), bf16), vm((count, width), f32),
            vm((2, dp, block, wide_d), bf16), vm((2, dp, block, wide_d), bf16), *sums, vm((rows, wide_d), bf16),
            *line(rs, width), *line(rs, width),
            vm((rows, RANK_LANES), f32), *sums_scratch, tile, tile, big, big, big,
            model, model, vm((rows, 2 * hidden), f32), vm((3, rows // 2, 2 * hidden), f32), *line(rs, 2 * hidden), vm((rows, hidden), f32), *line(rs, hidden),
            DMA((6,)), *both(dp), *both(dp), *both(rs - 1), *both(2, 2, rs), *both(2, 2, rs), *both(rs + 1),
            *both(2, 2, rs), *both(1), *both(rs - 1), *both(4, 2, rs), *both(2, 2, rs), *both(4, 2, rs), *both(6, 2),
        ],
        (
            x_in, cotangent, lengths, seq_order, norm1_gain, conv_taps, conv_b, w_xp, w_dt, dt_bias, rates, skip_weight,
            norm2_gain,
        ),
        (w_in_x, w_in_z, w_out, w_gate, w_up, w_down),
        leave=leave,
    )
    passed = dict(zip(leave, passed))
    first = ("dgu", "dot", "hid_all", "hid_mates", "cg", "cg_mates", "n2", "n2_mates")
    late = {name: passed[name] for name in (*first, *(name for name in passed if name not in first))}

    def sizes(value, parts):
        return vm((2, value[0] // parts, value[1]), bf16)

    def eighths(value):
        return vm((2, value[0] // 8, value[1]) if value in (d_cols, grads[5]) else (2, value[0] // 2, value[1] // 4), bf16)

    d_cols, f_cols, e_cols = (rs * hidden, wide_d), (wide_d, rs * hidden), (wide_d, rs * width)
    grads = (d_cols, f_cols, f_cols, e_cols, e_cols, (rs * width, wide_d), (2 * RANK_LANES, width))
    returned = in_vmem(
        functools.partial(backward_kernel, rank=rank, model_width=model_width),
        "backward",
        1,
        [((block, wide_d), bf16), ((block, wide_d), bf16)],
        [
            weight(w_gate), weight(w_up), weight(w_down), weight(w_out), weight(w_in_x), weight(w_in_z),
            vm((RANK_LANES, width), bf16), vm((count, width), f32),
            vm((rows, rs * hidden), bf16), vm((rows, rs * hidden), bf16),
            vm((rows, rs * width), bf16), vm((rows, rs * width), bf16),
            model, vm((rows, wide_d), bf16), vm((rows, wide_d), bf16), vm((rows, wide_d), bf16),
            vm((2, dp, block, wide_d), bf16), vm((2, dp, block, wide_d), bf16),
            model, model, model, model, vm((rs - 1, 8, rows), f32), vm((8, rows), f32), vm((8, rows), f32),
            vm((8, rows), f32), big, *line(rs, width),
            vm((rows + 1, count, width), f32), tile, tile, tile, tile,
            big, big, big, big, big, big, big, vm((rows, RANK_LANES), f32), *sums_scratch, vm((rows, RANK_LANES), f32),
            *[vm(value, bf16) for value in grads],
            *[vm((2, rows, max(value) // 4), bf16) for value in grads[1:5]], sizes(grads[6], 4),
            *[eighths(value) for value in grads[:6]], sizes(grads[6], 8),
            *[eighths(value) for value in grads[:6]], vm((2, rows, wide_d), bf16),
            DMA((6,)), *both(2, 2, rs), *both(2, 2, rs), *both(5), *both(rs - 1), *both(dp), *both(dp), *both(2, 2, rs),
            *both(rs - 1), *both(rs + 1), *both(2, 2, rs), *both(rs - 1), *both(len(grads), 5, 2),
            pltpu.SemaphoreType.REGULAR((len(grads), 2)), DMA((len(grads),)),
        ],
        (
            lengths, seq_order, norm2_gain, conv_taps, conv_b, w_xp, w_dt, dt_bias, rates, skip_weight, norm1_gain,
        ),
        (w_gate, w_up, w_down, w_out, w_in_x, w_in_z),
        [(value, bf16) for value in (grads[-1], *grads[:-1])],
        late,
    )
    steps = 2

    def pieces(value):
        return pl.BlockSpec((value[0] // steps, value[1]), lambda i: (i, 0))

    def whole(*shape):
        return pl.BlockSpec(shape, lambda i: (0,) * len(shape))

    rows_spec = whole(block, wide_d)
    shape = jax.ShapeDtypeStruct
    outs = (
        (rows_spec, (block, wide_d), bf16), (rows_spec, (block, wide_d), bf16), (whole(wide_d), (wide_d,), f32),
        (pieces(e_cols), e_cols, f32), (pieces(e_cols), e_cols, f32), (whole(taps, width), (taps, width), f32),
        (whole(width), (width,), f32), (whole(width, RANK_LANES), (width, RANK_LANES), f32),
        (whole(rank, width), (rank, width), f32), (whole(width), (width,), f32),
        (whole(count, width), (count, width), f32), (whole(width), (width,), f32), (pieces(grads[5]), grads[5], f32),
        (whole(wide_d), (wide_d,), f32), (pieces(f_cols), f_cols, f32), (pieces(f_cols), f_cols, f32),
        (pieces(d_cols), d_cols, f32),
    )
    results = pl.pallas_call(
        functools.partial(finish_kernel, rank=rank),
        grid=(steps,),
        in_specs=[rows_spec, rows_spec, whole(2 * RANK_LANES, width), *[pieces(value) for value in grads[:-1]]],
        out_specs=tuple(spec for spec, _, _ in outs),
        out_shape=tuple(shape(size, kind) for _, size, kind in outs),
        compiler_params=pltpu.CompilerParams(vmem_limit_bytes=VMEM_BYTES),
        name="finish",
    )(*returned)
    (y_out, dx_out, norm1, g_z, g_x, g_taps, g_bias, g_xp, g_dt, g_dt_bias, g_rate, g_skip, g_out, norm2, g_gate, g_up,
     g_down) = results
    return (
        y_out, dx_out, norm1, g_x, g_z, g_taps.T, g_bias, g_xp, g_dt, g_dt_bias, g_rate.T, g_skip, g_out, norm2,
        g_gate, g_up, g_down,
    )


def on_device(
    x_in,
    lengths,
    seq_order,
    norm1_gain,
    w_in_x,
    w_in_z,
    conv_w,
    conv_b,
    w_xp,
    w_dt,
    dt_bias,
    a_log,
    skip_weight,
    w_out,
    norm2_gain,
    w_gate,
    w_up,
    w_down,
    cotangent,
):
    rows_in, width_row = x_in.shape
    row_devices = lax.axis_size("row")
    col_devices = lax.axis_size("col")
    group_rows = rows_in * col_devices
    model_width = width_row * row_devices
    rank_cols = w_dt.shape[0]
    state_count = a_log.shape[1]
    channels = conv_w.shape[0]
    ff_cols = w_gate.shape[1]
    my_group = lax.axis_index("dp")
    my_column = lax.axis_index("col")
    source, position_all = layout(lengths, seq_order, group_rows)
    my_source = lax.dynamic_index_in_dim(source, my_group, 0, keepdims=False)
    position = lax.dynamic_index_in_dim(position_all, my_group, 0, keepdims=False)
    slice_source = lax.dynamic_slice_in_dim(my_source, my_column * rows_in, rows_in, 0)

    def row_total(values):
        return lax.psum(values, "row")

    def token_rows(values):
        return lax.all_gather(values, "col", axis=0, tiled=True)

    def row_pieces(values):
        return lax.all_gather(values, "row", axis=0, tiled=True)

    def col_reduce(term_fn):
        return lax.psum_scatter(
            term_fn(jnp.int32(0), lax.axis_size("col") * rows_in),
            "col",
            scatter_dimension=0,
            tiled=True,
        )

    def row_reduce(term_fn, keep_rows):
        return lax.psum_scatter(
            term_fn(jnp.int32(0), lax.axis_size("row") * keep_rows),
            "row",
            scatter_dimension=0,
            tiled=True,
        )

    def projection_total(values):
        return lax.psum(values, ("row", "col"))

    blank_rows = jnp.zeros((rows_in, width_row), jnp.bfloat16)
    pieces = (
        lax.all_gather(x_in, ("dp", "col"), axis=0, tiled=True),
        lax.all_gather(cotangent, ("dp", "col"), axis=0, tiled=True),
    )
    row_count = pieces[0].shape[0]
    offset = slice_source
    inside = ((offset >= 0) & (offset < row_count))[:, None]
    index = jnp.clip(offset, 0, row_count - 1)
    x_rows = jnp.where(inside, jnp.take(pieces[0], index, axis=0), blank_rows)
    cot_rows = jnp.where(inside, jnp.take(pieces[1], index, axis=0), blank_rows)
    x_val = x_rows.astype(jnp.float32)
    scale_one = lax.rsqrt(row_total(jnp.sum(x_val * x_val, axis=1)) / model_width + epsilon)
    normed_one = (x_val * scale_one[:, None] * norm1_gain[None, :]).astype(jnp.bfloat16)
    normed_all = token_rows(normed_one)

    def inner_term(begin_row, row_count):
        return jnp.concatenate(
            [contract(w_in_x, normed_all, 0, 1), contract(w_in_z, normed_all, 0, 1)], axis=1
        )

    inner = row_reduce(inner_term, channels)
    inner_x = inner[:, :group_rows]
    inner_z = inner[:, group_rows:]

    def conv_part(values, kernel, kernel_bias):
        return convolve(values, kernel, kernel_bias, position)

    conv_out, conv_pull = jax.vjp(conv_part, inner_x, conv_w, conv_b)
    u_low = conv_out.astype(jnp.bfloat16)
    u_val = u_low.astype(jnp.float32)
    projected = projection_total(contract(w_xp, u_low, 0, 0))
    step_low = projected[:rank_cols].astype(jnp.bfloat16)
    pre_step = contract(w_dt, step_low, 0, 0) + dt_bias[:, None]
    step_size = jax.nn.softplus(pre_step)

    decay_rate = -jnp.exp(a_log).T
    proj_rows = projected.T
    u_rows = u_val.T
    step_rows = step_size.T
    gone_rows = jnp.where(position[:, None] > 0, step_rows, 1e30)
    drive_rows = step_rows * u_rows
    at_b, at_c = rank_cols, rank_cols + state_count
    scanned = scan_alone(proj_rows, gone_rows, drive_rows, decay_rate, at_b, at_c)
    mixer_y = scanned.T + skip_weight[:, None] * u_val
    gated = mixer_y * jax.nn.silu(inner_z)
    gated_low = gated.astype(jnp.bfloat16)
    gated_all = row_pieces(gated_low)

    def mix_term(begin_row, row_count):
        return contract(gated_all, w_out, 0, 0)

    first_sum = x_val + col_reduce(mix_term)
    scale_two = lax.rsqrt(row_total(jnp.sum(first_sum * first_sum, axis=1)) / model_width + epsilon)
    normed_two = (first_sum * scale_two[:, None] * norm2_gain[None, :]).astype(jnp.bfloat16)
    normed_rows = token_rows(normed_two)

    def ffn_term(begin_row, row_count):
        return jnp.concatenate(
            [
                jnp.dot(normed_rows, w_gate, preferred_element_type=jnp.float32),
                jnp.dot(normed_rows, w_up, preferred_element_type=jnp.float32),
            ],
            axis=1,
        )

    gate_up = row_reduce(ffn_term, group_rows // row_devices)
    gate_val = gate_up[:, :ff_cols]
    up_val = gate_up[:, ff_cols:]
    hidden = (jax.nn.silu(gate_val) * up_val).astype(jnp.bfloat16)
    hidden_all = row_pieces(hidden)

    def down_term(begin_row, row_count):
        return jnp.dot(hidden_all, w_down, preferred_element_type=jnp.float32)

    second_sum = first_sum + col_reduce(down_term)
    out_low = second_sum.astype(jnp.bfloat16)
    back_down_all = token_rows(cot_rows)
    grad_down = contract(hidden_all, back_down_all, 0, 0)

    def hidden_term(begin_row, row_count):
        return contract(back_down_all, w_down, 1, 1)

    d_hidden = row_reduce(hidden_term, group_rows // row_devices)
    d_gate = (d_hidden * up_val * silu_slope(gate_val)).astype(jnp.bfloat16)
    d_up = (d_hidden * jax.nn.silu(gate_val)).astype(jnp.bfloat16)
    d_gate_up_all = row_pieces(jnp.concatenate([d_gate, d_up], axis=1))
    grad_gate = contract(normed_rows, d_gate_up_all[:, :ff_cols], 0, 0)
    grad_up = contract(normed_rows, d_gate_up_all[:, ff_cols:], 0, 0)

    def norm_two_term(begin_row, row_count):
        return contract(d_gate_up_all[:, :ff_cols], w_gate, 1, 1) + contract(
            d_gate_up_all[:, ff_cols:], w_up, 1, 1
        )

    d_normed_two = col_reduce(norm_two_term)
    cot_val = cot_rows.astype(jnp.float32)
    weighted_two = d_normed_two * norm2_gain[None, :]
    grad_norm_two = jnp.sum(d_normed_two * first_sum * scale_two[:, None], axis=0)
    dot_two = row_total(jnp.sum(weighted_two * first_sum, axis=1))
    d_first = (
        cot_val
        + scale_two[:, None] * weighted_two
        - first_sum * (scale_two**3 * dot_two / model_width)[:, None]
    )
    d_mix_all = token_rows(d_first.astype(jnp.bfloat16))
    grad_out = contract(gated_all, d_mix_all, 1, 0)

    def gated_term(begin_row, row_count):
        return contract(w_out, d_mix_all, 1, 1)

    d_gated = row_reduce(gated_term, channels)
    d_inner_z = d_gated * mixer_y * silu_slope(inner_z)
    d_mixer = d_gated * jax.nn.silu(inner_z)
    d_u_rows, d_step_rows, d_proj_rows, grad_rate_rows = adjoint_alone(
        proj_rows, step_rows, gone_rows, drive_rows, u_rows, d_mixer.T, decay_rate, at_b, at_c
    )
    d_u_mix = d_u_rows.T + skip_weight[:, None] * d_mixer
    d_step = d_step_rows.T
    d_enter = d_proj_rows.T[at_b:at_c]
    d_leave = d_proj_rows.T[at_c:]
    grad_rate = grad_rate_rows.T
    grad_skip = jnp.sum(d_mixer * u_val, axis=1)
    d_pre = d_step * jax.nn.sigmoid(pre_step)
    grad_step_bias = jnp.sum(d_pre, axis=1)
    d_pre_low = d_pre.astype(jnp.bfloat16)
    grad_step_w = contract(step_low, d_pre_low, 1, 1)
    d_projected = projection_total(
        jnp.concatenate(
            [jnp.dot(w_dt, d_pre_low, preferred_element_type=jnp.float32), d_enter, d_leave], axis=0
        )
    )
    d_proj_low = d_projected.astype(jnp.bfloat16)
    grad_proj_w = contract(u_low, d_proj_low, 1, 1)
    d_u_all = d_u_mix + jnp.dot(w_xp, d_proj_low, preferred_element_type=jnp.float32)
    d_inner_x, grad_kernel, grad_kernel_bias = conv_pull(d_u_all)
    d_inner_all = row_pieces(
        jnp.concatenate([d_inner_x.astype(jnp.bfloat16), d_inner_z.astype(jnp.bfloat16)], axis=1)
    )
    grad_in_x = contract(normed_all, d_inner_all[:, :group_rows], 0, 1)
    grad_in_z = contract(normed_all, d_inner_all[:, group_rows:], 0, 1)

    def norm_one_term(begin_row, row_count):
        piece_x = lax.dynamic_slice_in_dim(d_inner_all, begin_row, row_count, 1)
        piece_z = lax.dynamic_slice_in_dim(d_inner_all, group_rows, row_count, 1)
        return contract(piece_x, w_in_x, 0, 1) + contract(piece_z, w_in_z, 0, 1)

    d_normed_one = col_reduce(norm_one_term)
    weighted_one = d_normed_one * norm1_gain[None, :]
    grad_norm_one = jnp.sum(d_normed_one * x_val * scale_one[:, None], axis=0)
    dot_one = row_total(jnp.sum(weighted_one * x_val, axis=1))
    d_input = (
        d_first
        + scale_one[:, None] * weighted_one
        - x_val * (scale_one**3 * dot_one / model_width)[:, None]
    )
    d_input_low = d_input.astype(jnp.bfloat16)
    grad_norm_one, grad_norm_two = lax.psum((grad_norm_one, grad_norm_two), ("dp", "col"))
    (
        grad_in_x,
        grad_in_z,
        grad_kernel,
        grad_kernel_bias,
        grad_proj_w,
        grad_step_w,
        grad_step_bias,
        grad_rate,
        grad_skip,
        grad_out,
        grad_gate,
        grad_up,
        grad_down,
    ) = (
        lax.psum(grad_in_x.astype(jnp.bfloat16), "dp").astype(jnp.float32),
        lax.psum(grad_in_z.astype(jnp.bfloat16), "dp").astype(jnp.float32),
        lax.psum(grad_kernel.astype(jnp.bfloat16), "dp").astype(jnp.float32),
        lax.psum(grad_kernel_bias.astype(jnp.bfloat16), "dp").astype(jnp.float32),
        lax.psum(grad_proj_w.astype(jnp.bfloat16), "dp").astype(jnp.float32),
        lax.psum(grad_step_w.astype(jnp.bfloat16), "dp").astype(jnp.float32),
        lax.psum(grad_step_bias.astype(jnp.bfloat16), "dp").astype(jnp.float32),
        lax.psum(grad_rate.astype(jnp.bfloat16), "dp").astype(jnp.float32),
        lax.psum(grad_skip.astype(jnp.bfloat16), "dp").astype(jnp.float32),
        lax.psum(grad_out.astype(jnp.bfloat16), "dp").astype(jnp.float32),
        lax.psum(grad_gate.astype(jnp.bfloat16), "dp").astype(jnp.float32),
        lax.psum(grad_up.astype(jnp.bfloat16), "dp").astype(jnp.float32),
        lax.psum(grad_down.astype(jnp.bfloat16), "dp").astype(jnp.float32),
    )
    payload = jnp.concatenate([out_low, d_input_low], axis=1)
    tokens_all = lengths.shape[0] * group_rows
    owner = (
        jnp.zeros((tokens_all,), jnp.int32)
        .at[source.reshape(-1)]
        .set(jnp.arange(tokens_all, dtype=jnp.int32))
    )
    my_rows = lax.dynamic_slice_in_dim(
        owner, (my_group * col_devices + my_column) * rows_in, rows_in, 0
    )
    pieces = lax.all_gather(payload, ("dp", "col"), axis=0, tiled=True)
    row_count = pieces.shape[0]
    offset = my_rows
    inside = ((offset >= 0) & (offset < row_count))[:, None]
    returned = jnp.where(
        inside,
        jnp.take(pieces, jnp.clip(offset, 0, row_count - 1), axis=0),
        jnp.zeros_like(payload),
    )
    y_out = returned[:, :width_row]
    dx_out = returned[:, width_row:]
    return (
        y_out,
        dx_out,
        grad_norm_one,
        grad_in_x,
        grad_in_z,
        grad_kernel,
        grad_kernel_bias,
        grad_proj_w,
        grad_step_w,
        grad_step_bias,
        grad_rate,
        grad_skip,
        grad_out,
        grad_norm_two,
        grad_gate,
        grad_up,
        grad_down,
    )


def solution(mesh):
    placed = (
        P(("dp", "col"), "row"),
        P(),
        P(),
        P("row"),
        P("row", "col"),
        P("row", "col"),
        P(("col", "row"), None),
        P(("col", "row")),
        P(("col", "row"), None),
        P(None, ("col", "row")),
        P(("col", "row")),
        P(("col", "row"), None),
        P(("col", "row")),
        P("col", "row"),
        P("row"),
        P("row", "col"),
        P("row", "col"),
        P("col", "row"),
        P(("dp", "col"), "row"),
    )
    paired = mesh.shape["col"] == 2 and mesh.shape["dp"] == 4
    return jax.shard_map(
        on_pairs if paired else on_device,
        mesh=mesh,
        in_specs=placed,
        out_specs=(
            P(("dp", "col"), "row"),
            P(("dp", "col"), "row"),
            P("row"),
            P("row", "col"),
            P("row", "col"),
            P(("col", "row"), None),
            P(("col", "row")),
            P(("col", "row"), None),
            P(None, ("col", "row")),
            P(("col", "row")),
            P(("col", "row"), None),
            P(("col", "row")),
            P("col", "row"),
            P("row"),
            P("row", "col"),
            P("row", "col"),
            P("col", "row"),
        ),
        check_vma=False,
    )
```

profile of v0, /device:TPU:0, one launch (start us, length us, event | category | flops | bytes accessed | tf_op | source)
XLA Modules:
  0.0 285.2 jit_solution(7872124745089923545)
XLA Ops:
  0.7 134.4 %forward.1 = (bf16[256,384]{1,0:T(8,128)(2,1)}, bf16[256,384]{1,0:T(8,128)(2,1)}, bf16[256,384]{1,0:T(8,128)(2,1)}, f32[256,1]{1,0:T(8,128)}, f32[256,1]{1,0:T(8...) custom-call(bf16[128,384]{1,0:T(8,128)(2,1)} %refs_0_.2, ...), custom_call_target="tpu_custom_call" | custom-call | tf_op jit(solution)/shard_map/forward/pallas_call | solution.py:1420
  135.1 140.7 %backward.1 = (bf16[128,384]{1,0:T(8,128)(2,1)}, bf16[128,384]{1,0:T(8,128)(2,1)}, bf16[256,384]{1,0:T(8,128)(2,1)}, bf16[2048,384]{1,0:T(8,128)(2,1)}, bf16[384...) custom-call(s32[4,8]{1,0:T(4,128)} %refs_0_.3, ...), custom_call_target="tpu_custom_call" | custom-call | tf_op jit(solution)/shard_map/backward/pallas_call | solution.py:1420
  275.7 9.3 %finish.1 = (bf16[128,384]{1,0:T(8,128)(2,1)}, bf16[128,384]{1,0:T(8,128)(2,1)}, f32[384]{0:T(512)}, f32[384,1536]{1,0:T(8,128)}, f32[384,1536]{1,0:T(8,128)}, /...) custom-call(bf16[128,384]{1,0:T(8,128)(2,1)} %get-tuple-element.85.y, ...), custom_call_target="tpu_custom_call" | custom-call | tf_op jit(solution)/shard_map/finish/pallas_call | solution.py:1562
where the time goes:
time: 285 us
  Pallas kernels  284 us (100%)
    pallas_call x2, Pallas kernels, in_vmem(): pl.pallas_call(whole, out_shape=tuple((jax.ShapeDtypeStruct(shape, kind)...  275 us
    pallas_call x1, Pallas kernels, on_pairs(): pl.pallas_call(functools.partial(finish_kernel, rank=rank), grid=(steps,)...  9.3 us

commit v1 on v0

--- a/solution.py
+++ b/solution.py
@@ -669,7 +669,7 @@
     )(proj, step, gone, drive, inner_u, dy, rate)
 
 
-PUMPS = ((0, 1, 1), (1, 0, 1), 0, (1, 2, 1), (1, 1), (0, 0, 0), (2, 2, 1), 0, 2)
+PUMPS = ((0, 1, 1), (1, 1, 1), 0, (1, 2, 1), (1, 1), (0, 0, 0), (2, 2, 1), 0, 2)
 
 
 def conv_sum(inner_x, place, taps, bias):
@@ -960,14 +960,18 @@
             )
             self.back = (copy(3, there[0], there[0], mate), copy(4, there[1], there[1], mate))
 
-        def product(self):
-            mine, mates_part = sent[:, side(self.h, self.near)], sent_in[self.h]
+    def products():
+        def one(h, _):
+            near = jnp.where(h == 0, bits[0], bits[1])
+            here = side(h, near)
+            mine, mates_part, mates_fixed = sent[:, here], sent_in[h], fixed_mates[h]
             if by_rows:
-                found = over_rows(mine, fixed[...]) + over_rows(mates_part, fixed_mates[self.h])
-                grad[side(self.h, self.near), :] = found.astype(bf16)
+                grad[here, :] = (over_rows(mine, fixed[...]) + over_rows(mates_part, mates_fixed)).astype(bf16)
             else:
-                found = over_rows(fixed[...], mine) + over_rows(fixed_mates[self.h], mates_part)
-                grad[:, side(self.h, self.near)] = found.astype(bf16)
+                grad[:, here] = (over_rows(fixed[...], mine) + over_rows(mates_fixed, mates_part)).astype(bf16)
+            return 0
+
+        lax.fori_loop(0, 2, one, 0)
 
     both_halves = (Half(0), Half(1))
     if swapped:
@@ -977,7 +981,8 @@
     for half in both_halves:
         if swapped:
             half.out[0].wait_recv()
-        half.product()
+    products()
+    for half in both_halves:
         half.out[1].start()
     yield
     for half in both_halves:

time: 285 us -> 294 us (1.032)
  Pallas kernels: 284 us -> 293 us
    pallas_call x2, Pallas kernels: 275 us -> 283 us  [in_vmem(): pl.pallas_call(whole, out_shape=tuple((jax.ShapeDtypeStruct(shape, kind)...]
where the time goes in v1:
time: 294 us; the launch traced here: 293 us
  Pallas kernels  293 us (100%)
    pallas_call x2, Pallas kernels, in_vmem(): pl.pallas_call(whole, out_shape=tuple((jax.ShapeDtypeStruct(shape, kind)...  283 us
    pallas_call x1, Pallas kernels, on_pairs(): pl.pallas_call(functools.partial(finish_kernel, rank=rank), grid=(steps,)...  9.3 us

profile of v1, /device:TPU:0, one launch (start us, length us, event | category | flops | bytes accessed | tf_op | source)
XLA Modules:
  0.0 293.4 jit_solution(13918137101755480473)
XLA Ops:
  0.7 134.4 %forward.1 = (bf16[256,384]{1,0:T(8,128)(2,1)}, bf16[256,384]{1,0:T(8,128)(2,1)}, bf16[256,384]{1,0:T(8,128)(2,1)}, f32[256,1]{1,0:T(8,128)}, f32[256,1]{1,0:T(8...) custom-call(bf16[128,384]{1,0:T(8,128)(2,1)} %refs_0_.2, ...), custom_call_target="tpu_custom_call" | custom-call | tf_op jit(solution)/shard_map/forward/pallas_call | solution.py:1425
  135.1 148.8 %backward.1 = (bf16[128,384]{1,0:T(8,128)(2,1)}, bf16[128,384]{1,0:T(8,128)(2,1)}, bf16[256,384]{1,0:T(8,128)(2,1)}, bf16[2048,384]{1,0:T(8,128)(2,1)}, bf16[384...) custom-call(s32[4,8]{1,0:T(4,128)} %refs_0_.3, ...), custom_call_target="tpu_custom_call" | custom-call | tf_op jit(solution)/shard_map/backward/pallas_call | solution.py:1425
  283.9 9.3 %finish.1 = (bf16[128,384]{1,0:T(8,128)(2,1)}, bf16[128,384]{1,0:T(8,128)(2,1)}, f32[384]{0:T(512)}, f32[384,1536]{1,0:T(8,128)}, f32[384,1536]{1,0:T(8,128)}, /...) custom-call(bf16[128,384]{1,0:T(8,128)(2,1)} %get-tuple-element.85.y, ...), custom_call_target="tpu_custom_call" | custom-call | tf_op jit(solution)/shard_map/finish/pallas_call | solution.py:1567
